TPU v7x, 32 devices: a whole 2x2x4 slice. The times are simulated.
32 devices in a mesh: wide: 8 (over z, y), narrow: 4 (over x, core).
Axes of the slice: x: 2, y: 2, z: 4, core: 2. Of those that a mesh axis runs over, the one named last changes fastest.
Arguments:
- tokens: bfloat16 [64, 512, 768], P(('wide', 'narrow')), may hold values from -18 to 18
- mask_place: int32 [64, 76], P(('wide', 'narrow')), may hold values from 0 to 511, as said below
- mask_count: int32 [64], P(('wide', 'narrow')), may hold values from 38 to 76, as said below
- masked_output_gradient: bfloat16 [64, 76, 768], P(('wide', 'narrow')), may hold values from -6 to 6
- query_key_value_weight: float32 [3, 768, 768], P(None, 'wide'), may hold values from -0.15625 to 0.15625
- qkv_first: float32 [3, 768, 768], P(None, 'wide'), may hold values from -0.00061035156 to 0.00061035156
- qkv_second: float32 [3, 768, 768], P(None, 'wide'), may hold values from 1.4110135e-10 to 5.644054e-10
- out_weight: float32 [768, 768], P(None, 'wide'), may hold values from -1.25 to 1.25
- out_first: float32 [768, 768], P(None, 'wide'), may hold values from -0.00061035156 to 0.00061035156
- out_second: float32 [768, 768], P(None, 'wide'), may hold values from 1.4110135e-10 to 5.644054e-10
- up_weight: float32 [768, 3072], P('wide'), may hold values from -0.21875 to 0.21875
- up_first: float32 [768, 3072], P('wide'), may hold values from -0.00061035156 to 0.00061035156
- up_second: float32 [768, 3072], P('wide'), may hold values from 1.4110135e-10 to 5.644054e-10
- down_weight: float32 [3072, 768], P(None, 'wide'), may hold values from -0.109375 to 0.109375
- down_first: float32 [3072, 768], P(None, 'wide'), may hold values from -0.00061035156 to 0.00061035156
- down_second_moment: float32 [3072, 768], P(None, 'wide'), may hold values from 1.4110135e-10 to 5.644054e-10
- vectors: float32 [8, 768], P(None, 'wide'), may hold values from -1 to 3
- vectors_first: float32 [8, 768], P(None, 'wide'), may hold values from -0.00061035156 to 0.00061035156
- vectors_second: float32 [8, 768], P(None, 'wide'), may hold values from 1.4110135e-10 to 5.644054e-10
- up_bias: float32 [3072], P('wide'), may hold values from -3 to 3
- up_bias_first: float32 [3072], P('wide'), may hold values from -0.00061035156 to 0.00061035156
- up_bias_second: float32 [3072], P('wide'), may hold values from 1.4110135e-10 to 5.644054e-10
Outputs:
- layer_out: bfloat16 [64, 512, 768], P(('wide', 'narrow'))
- tokens_grad: float32 [64, 512, 768], P(('wide', 'narrow'))
- grad_norm: float32 [], replicated
- qkv_new: float32 [3, 768, 768], P(None, 'wide')
- qkv_first_new: float32 [3, 768, 768], P(None, 'wide')
- qkv_second_new: float32 [3, 768, 768], P(None, 'wide')
- out_new: float32 [768, 768], P(None, 'wide')
- out_first_new: float32 [768, 768], P(None, 'wide')
- out_second_new: float32 [768, 768], P(None, 'wide')
- up_new: float32 [768, 3072], P('wide')
- up_first_new: float32 [768, 3072], P('wide')
- up_second_new: float32 [768, 3072], P('wide')
- down_new: float32 [3072, 768], P(None, 'wide')
- down_first_new: float32 [3072, 768], P(None, 'wide')
- down_second_new: float32 [3072, 768], P(None, 'wide')
- updated_gain_vectors: float32 [8, 768], P(None, 'wide')
- vectors_first_new: float32 [8, 768], P(None, 'wide')
- vectors_second_new: float32 [8, 768], P(None, 'wide')
- up_bias_new: float32 [3072], P('wide')
- up_bias_first_new: float32 [3072], P('wide')
- up_bias_second_new: float32 [3072], P('wide')
Inputs may be any that keep to these rules, and one draw needn't show every extreme that they name: `mask_place`: the positions of one row are distinct; slots at and past the row's count are padding and carry no gradient. `mask_count`: some sequence uses all 76 slots.
All inputs are finite; a program needn't handle non-finite values.
Results may differ from a plain program's by a relative error of at most 0.02.
Values may be sent and summed in bfloat16 or wider, within the bound.
A program may use at most 256 MiB of HBM per device.

v0:
```python
import jax
import jax.numpy as jnp
from jax import lax
from jax.sharding import PartitionSpec as P

HEADS = 12
HEAD_DIM = 64
STEP = 10


LN_EPS = 1e-06
SQRT_HALF = 0.7071067811865476
INV_ROOT_TWO_PI = 0.3989422804014327
CLIP_LIMIT = 1.0
BETA_ONE = 0.9
BETA_TWO = 0.999
LEARN_RATE = 0.05
OUTPUT_RATE = 0.2
VECTOR_RATE = 0.5
BIAS_RATE = 0.3
DECAY_RATE = 0.01
ADAM_EPS = 1e-08


def layer_norm(values, gain, shift):
    center = values - jnp.mean(values, axis=-1, keepdims=True)
    inverse = lax.rsqrt(jnp.mean(center * center, axis=-1, keepdims=True) + LN_EPS)
    normed = center * inverse
    return (normed * gain + shift, normed, inverse)


def norm_back(incoming, normed, inverse, gain):
    dgain = jnp.sum(incoming * normed, axis=0)
    dshift = jnp.sum(incoming, axis=0)
    scaled = incoming * gain
    dvalues = inverse * (
        scaled
        - jnp.mean(scaled, axis=-1, keepdims=True)
        - normed * jnp.mean(scaled * normed, axis=-1, keepdims=True)
    )
    return (dvalues, dgain, dshift)


def split_heads(values, seqs, length):
    return values.reshape(seqs, length, HEADS, HEAD_DIM)


def attend(pieces):
    query, key, value = pieces
    raw = jnp.einsum("qhe,khe->hqk", query, key, preferred_element_type=jnp.float32) * HEAD_DIM ** (
        -0.5
    )
    peak = jnp.max(raw, axis=-1, keepdims=True)
    expo = jnp.exp(raw - peak)
    total = jnp.sum(expo, axis=-1, keepdims=True)
    probs = (expo / total).astype(jnp.bfloat16)
    mixed = jnp.einsum("hqk,khe->qhe", probs, value, preferred_element_type=jnp.float32)
    return (mixed.astype(jnp.bfloat16), (peak + jnp.log(total))[..., 0])


def attend_back(pieces):
    query, key, value, logsum, dmixed = pieces
    scale = HEAD_DIM ** (-0.5)
    raw = jnp.einsum("qhe,khe->hqk", query, key, preferred_element_type=jnp.float32) * scale
    probs = jnp.exp(raw - logsum[..., None])
    dprobs = jnp.einsum("qhe,khe->hqk", dmixed, value, preferred_element_type=jnp.float32)
    dscore = probs * (dprobs - jnp.sum(dprobs * probs, axis=-1, keepdims=True))
    dscore = (dscore * scale).astype(jnp.bfloat16)
    dquery = jnp.einsum("hqk,khe->qhe", dscore, key, preferred_element_type=jnp.float32)
    dkey = jnp.einsum("hqk,qhe->khe", dscore, query, preferred_element_type=jnp.float32)
    dvalue = jnp.einsum(
        "hqk,qhe->khe", probs.astype(jnp.bfloat16), dmixed, preferred_element_type=jnp.float32
    )
    return (dquery, dkey, dvalue)


def adam_step(weight, first, second, grad, factor, decay, rate):
    grad = grad * factor
    first_new = BETA_ONE * first + (1.0 - BETA_ONE) * grad
    second_new = BETA_TWO * second + (1.0 - BETA_TWO) * grad * grad
    mean_hat = first_new / (1.0 - BETA_ONE**STEP)
    square_hat = second_new / (1.0 - BETA_TWO**STEP)
    weight_new = weight - rate * (mean_hat / (jnp.sqrt(square_hat) + ADAM_EPS) + decay * weight)
    return (weight_new, first_new, second_new)


def shards(
    tokens,
    mask_place,
    mask_count,
    masked_output_gradient,
    query_key_value_weight,
    qkv_first,
    qkv_second,
    out_weight,
    out_first,
    out_second,
    up_weight,
    up_first,
    up_second,
    down_weight,
    down_first,
    down_second_moment,
    vectors,
    vectors_first,
    vectors_second,
    up_bias,
    up_bias_first,
    up_bias_second,
):
    seqs, length, width = tokens.shape
    flat = tokens.reshape(seqs * length, width)
    qkv_full, out_full, vec_full = (
        lax.all_gather(query_key_value_weight.astype(jnp.bfloat16), "wide", axis=1, tiled=True),
        lax.all_gather(out_weight.astype(jnp.bfloat16), "wide", axis=1, tiled=True),
        lax.all_gather(vectors.astype(jnp.bfloat16), "wide", axis=1, tiled=True),
    )
    up_full, down_full, bias_full = (
        lax.all_gather(up_weight.astype(jnp.bfloat16), "wide", axis=0, tiled=True),
        lax.all_gather(down_weight.astype(jnp.bfloat16), "wide", axis=1, tiled=True),
        lax.all_gather(up_bias.astype(jnp.bfloat16), "wide", axis=0, tiled=True),
    )
    vec_vals = vec_full.astype(jnp.float32)
    proj = jnp.einsum("td,kde->kte", flat, qkv_full, preferred_element_type=jnp.float32)
    query = split_heads((proj[0] + vec_vals[0]).astype(jnp.bfloat16), seqs, length)
    key = split_heads(proj[1].astype(jnp.bfloat16), seqs, length)
    value = split_heads((proj[2] + vec_vals[1]).astype(jnp.bfloat16), seqs, length)
    mixed, logsum = lax.map(attend, (query, key, value))
    mixed = mixed.reshape(seqs * length, width)
    pre_one = flat.astype(jnp.float32) + (
        jnp.dot(mixed, out_full, preferred_element_type=jnp.float32) + vec_vals[2]
    )
    hidden, normed_one, inverse_one = layer_norm(pre_one, vec_vals[3], vec_vals[4])
    hidden_low = hidden.astype(jnp.bfloat16)
    upper = jnp.dot(hidden_low, up_full, preferred_element_type=jnp.float32) + bias_full.astype(
        jnp.float32
    )
    cumul = 0.5 * (1.0 + lax.erf(upper * SQRT_HALF))
    active = (upper * cumul).astype(jnp.bfloat16)
    pre_two = hidden + (
        jnp.dot(active, down_full, preferred_element_type=jnp.float32) + vec_vals[5]
    )
    layer_result, normed_two, inverse_two = layer_norm(pre_two, vec_vals[6], vec_vals[7])
    slots = jnp.arange(mask_place.shape[1])
    valid = slots[None, :] < mask_count[:, None]
    masked_positions = (
        (mask_place[:, :, None] == jnp.arange(length)[None, None, :]) & valid[:, :, None]
    ).astype(jnp.bfloat16)
    dresult = jnp.einsum(
        "xir,xin->xrn", masked_positions, masked_output_gradient, preferred_element_type=jnp.float32
    ).reshape(seqs * length, width)
    dpre_two, dgain_two, dshift_two = norm_back(dresult, normed_two, inverse_two, vec_vals[6])
    up_back, down_back = (
        lax.all_gather(up_weight.astype(jnp.bfloat16), "wide", axis=0, tiled=True),
        lax.all_gather(down_weight.astype(jnp.bfloat16), "wide", axis=1, tiled=True),
    )
    dbias_two = jnp.sum(dpre_two, axis=0)
    dtwo_low = dpre_two.astype(jnp.bfloat16)
    ddown = jnp.einsum("tf,td->fd", active, dtwo_low, preferred_element_type=jnp.float32)
    dactive = jnp.einsum("td,fd->tf", dtwo_low, down_back, preferred_element_type=jnp.float32)
    density = jnp.exp(-0.5 * upper * upper) * INV_ROOT_TWO_PI
    dupper = dactive * (cumul + upper * density)
    dup_bias = jnp.sum(dupper, axis=0)
    dupper_low = dupper.astype(jnp.bfloat16)
    dup = jnp.einsum("td,tf->df", hidden_low, dupper_low, preferred_element_type=jnp.float32)
    dhidden = dpre_two + jnp.einsum(
        "tf,df->td", dupper_low, up_back, preferred_element_type=jnp.float32
    )
    own_up, own_down, own_bias = (
        lax.psum_scatter(dup, "wide", scatter_dimension=0, tiled=True),
        lax.psum_scatter(ddown, "wide", scatter_dimension=1, tiled=True),
        lax.psum_scatter(dup_bias, "wide", scatter_dimension=0, tiled=True),
    )
    dpre_one, dgain_one, dshift_one = norm_back(dhidden, normed_one, inverse_one, vec_vals[3])
    qkv_back, out_back = (
        lax.all_gather(query_key_value_weight.astype(jnp.bfloat16), "wide", axis=1, tiled=True),
        lax.all_gather(out_weight.astype(jnp.bfloat16), "wide", axis=1, tiled=True),
    )
    dbias_out = jnp.sum(dpre_one, axis=0)
    done_low = dpre_one.astype(jnp.bfloat16)
    dout_weight = jnp.einsum("te,td->ed", mixed, done_low, preferred_element_type=jnp.float32)
    dmixed = jnp.einsum("td,ed->te", done_low, out_back, preferred_element_type=jnp.float32).astype(
        jnp.bfloat16
    )
    dquery, dkey, dvalue = lax.map(
        attend_back, (query, key, value, logsum, split_heads(dmixed, seqs, length))
    )
    dquery = dquery.reshape(seqs * length, width)
    dkey = dkey.reshape(seqs * length, width)
    dvalue = dvalue.reshape(seqs * length, width)
    query_bias_gradient = jnp.sum(dquery, axis=0)
    dbias_value = jnp.sum(dvalue, axis=0)
    dstack = jnp.stack([dquery, dkey, dvalue]).astype(jnp.bfloat16)
    dqkv = jnp.einsum("td,kte->kde", flat, dstack, preferred_element_type=jnp.float32)
    dtokens = dpre_one + jnp.einsum(
        "kte,kde->td", dstack, qkv_back, preferred_element_type=jnp.float32
    )
    dvectors = jnp.stack(
        [
            query_bias_gradient,
            dbias_value,
            dbias_out,
            dgain_one,
            dshift_one,
            dbias_two,
            dgain_two,
            dshift_two,
        ]
    )
    own_qkv, own_out, own_vectors = (
        lax.psum_scatter(dqkv, "wide", scatter_dimension=1, tiled=True),
        lax.psum_scatter(dout_weight, "wide", scatter_dimension=1, tiled=True),
        lax.psum_scatter(dvectors, "wide", scatter_dimension=1, tiled=True),
    )
    own_qkv, own_out, own_up, own_down, own_vectors, own_bias = (
        lax.psum(own_qkv.astype(jnp.bfloat16), "narrow").astype(jnp.float32),
        lax.psum(own_out.astype(jnp.bfloat16), "narrow").astype(jnp.float32),
        lax.psum(own_up.astype(jnp.bfloat16), "narrow").astype(jnp.float32),
        lax.psum(own_down.astype(jnp.bfloat16), "narrow").astype(jnp.float32),
        lax.psum(own_vectors.astype(jnp.bfloat16), "narrow").astype(jnp.float32),
        lax.psum(own_bias.astype(jnp.bfloat16), "narrow").astype(jnp.float32),
    )
    partial_squares = (
        jnp.sum(own_qkv * own_qkv)
        + jnp.sum(own_out * own_out)
        + jnp.sum(own_up * own_up)
        + jnp.sum(own_down * own_down)
        + jnp.sum(own_vectors * own_vectors)
        + jnp.sum(own_bias * own_bias)
    )
    total_squares = lax.psum(partial_squares, "wide")
    grad_norm = jnp.sqrt(total_squares)
    factor = CLIP_LIMIT / jnp.maximum(grad_norm, CLIP_LIMIT)
    qkv_n, qkv_m, qkv_v = adam_step(
        query_key_value_weight, qkv_first, qkv_second, own_qkv, factor, DECAY_RATE, LEARN_RATE
    )
    out_n, out_m, out_v = adam_step(
        out_weight, out_first, out_second, own_out, factor, DECAY_RATE, OUTPUT_RATE
    )
    up_n, up_m, up_v = adam_step(
        up_weight, up_first, up_second, own_up, factor, DECAY_RATE, LEARN_RATE
    )
    down_n, down_m, down_v = adam_step(
        down_weight, down_first, down_second_moment, own_down, factor, DECAY_RATE, LEARN_RATE
    )
    vec_n, vec_m, vec_v = adam_step(
        vectors, vectors_first, vectors_second, own_vectors, factor, 0.0, VECTOR_RATE
    )
    bias_n, bias_m, bias_v = adam_step(
        up_bias, up_bias_first, up_bias_second, own_bias, factor, 0.0, BIAS_RATE
    )
    layer_out = layer_result.astype(jnp.bfloat16).reshape(seqs, length, width)
    tokens_grad = dtokens.reshape(seqs, length, width)
    return (
        layer_out,
        tokens_grad,
        grad_norm,
        qkv_n,
        qkv_m,
        qkv_v,
        out_n,
        out_m,
        out_v,
        up_n,
        up_m,
        up_v,
        down_n,
        down_m,
        down_v,
        vec_n,
        vec_m,
        vec_v,
        bias_n,
        bias_m,
        bias_v,
    )


def solution(mesh):
    in_specs = (
        P(("wide", "narrow"), None, None),
        P(("wide", "narrow"), None),
        P(("wide", "narrow")),
        P(("wide", "narrow"), None, None),
        P(None, "wide", None),
        P(None, "wide", None),
        P(None, "wide", None),
        P(None, "wide"),
        P(None, "wide"),
        P(None, "wide"),
        P("wide", None),
        P("wide", None),
        P("wide", None),
        P(None, "wide"),
        P(None, "wide"),
        P(None, "wide"),
        P(None, "wide"),
        P(None, "wide"),
        P(None, "wide"),
        P("wide"),
        P("wide"),
        P("wide"),
    )
    out_specs = (
        P(("wide", "narrow"), None, None),
        P(("wide", "narrow"), None, None),
        P(),
        P(None, "wide", None),
        P(None, "wide", None),
        P(None, "wide", None),
        P(None, "wide"),
        P(None, "wide"),
        P(None, "wide"),
        P("wide", None),
        P("wide", None),
        P("wide", None),
        P(None, "wide"),
        P(None, "wide"),
        P(None, "wide"),
        P(None, "wide"),
        P(None, "wide"),
        P(None, "wide"),
        P("wide"),
        P("wide"),
        P("wide"),
    )
    return jax.shard_map(shards, mesh=mesh, in_specs=in_specs, out_specs=out_specs, check_vma=False)
```

profile of v0, /device:TPU:0, one launch (start us, length us, event | category | flops | bytes accessed | tf_op | source)
XLA Modules:
  0.0 1146.5 jit_solution(10867617208058265949)
XLA Ops:
  13.3 27.8 %all-gather.1 = bf16[8,1,384]{2,1,0:T(2,128)(2,1)S(1)} all-gather(bf16[1,1,384]{2,1,0:T(2,128)(2,1)S(1)} %reshape.191), channel_id=1, replica_groups=mesh['wide'=8,'narrow'=4] {'wide'}, dimensions={0}, use_global_device_ids=true | all-gather | bytes 6912 | tf_op jit(solution)/shard_map/all_gather | solution.py:121
  41.2 26.5 %all-gather = bf16[8,96,8]{1,2,0:T(8,128)(2,1)S(1)} all-gather(bf16[1,96,8]{1,2,0:T(8,128)(2,1)S(1)} %convert_bitcast_fusion), channel_id=1, replica_groups=mesh['wide'=8,'narrow'=4] {'wide'}, dimensions={0}, use_global_device_ids=true | all-gather | bytes 13824 | tf_op jit(solution)/shard_map/all_gather | solution.py:116
  107.4 15.3 %while.26 = (s32[]{:T(128)}, bf16[2,512,12,64]{1,3,2,0:T(8,128)(2,1)}, f32[2,12,512]{2,1,0:T(8,128)S(1)}, bf16[2,512,12,64]{1,3,2,0:T(8,128)(2,1)}, bf16[2,512,1...) while((s32[]{:T(128)}, bf16[2,512,12,64]{1,3,2,0:T(8,128)(2,1)}, ...), condition=%wide.region_3.4_spmd, body=%wide.region_0.3_spmd.sunk | while | flops 834004992 | bytes 47425652 | solution.py:128
  133.4 69.5 %all-gather.11.cloned.1.call-done = bf16[768,3072]{1,0:T(8,128)(2,1)} async-done(((bf16[96,3072]{1,0:T(8,128)(2,1)}), bf16[768,3072]{1,0:T(8,128)(2,1)}) %all-gather.11.cloned.1.call-update) | async-done | bytes 4718608 | tf_op jit(solution)/shard_map/all_gather | solution.py:119
  202.9 12.6 %multiply_convert_fusion.1 = (bf16[1024,3072]{1,0:T(8,128)(2,1)}, f32[1024,3072]{1,0:T(8,128)}) fusion(f32[3072]{0:T(1024)S(1)} %bitcast.171, bf16[768,3072]{1,0:T(8,128)(2,1)} %all-gather.11.cloned.1.call-done, f32[1024,768]{1,0:T(8,128)} %copy-done.4, f32[768]{0:T(1024)S(1)} %get-tuple-element.227, f32[768]{0:T(1024)S(1)} %get-tuple-element.228, ...), kind=kOutput, calls=%fused_computation.70 | convolution fusion | flops 4854644736 | bytes 26765312 | tf_op jit(solution)/shard_map/dot_general | solution.py:135
  215.6 68.0 %all-gather.13.cloned.1.call-done = bf16[3072,768]{0,1:T(8,128)(2,1)} async-done(((bf16[3072,96]{0,1:T(8,128)(2,1)}), bf16[3072,768]{0,1:T(8,128)(2,1)}) %all-gather.13.cloned.1.call-update) | async-done | bytes 4718608 | tf_op jit(solution)/shard_map/all_gather | solution.py:120
  299.7 13.8 %fusion.150 = (f32[3072]{0:T(1024)}, bf16[1024,3072]{1,0:T(8,128)(2,1)S(1)}) fusion(f32[1024,3072]{1,0:T(8,128)} %get-tuple-element.302, f32[3072]{0:T(1024)S(1)} %bitcast.172, bf16[3072,768]{0,1:T(8,128)(2,1)} %all-gather.13.cloned.1.call-done, f32[1024,768]{1,0:T(8,128)S(1)} %get-tuple-element.287), kind=kOutput, calls=%fused_computation.197 | convolution fusion | flops 4870370304 | bytes 26763264 | tf_op jit(solution)/shard_map/td,fd->tf/dot_general | solution.py:160
  340.4 106.8 %while.27 = (s32[]{:T(128)}, f32[2,512,12,64]{1,3,2,0:T(8,128)}, bf16[2,512,12,64]{1,3,2,0:T(8,128)(2,1)}, f32[2,512,12,64]{1,3,2,0:T(8,128)}, bf16[2,512,12,64]...) while((s32[]{:T(128)}, f32[2,512,12,64]{1,3,2,0:T(8,128)}, ...), condition=%wide.region_14.15_spmd, body=%wide.region_12.14_spmd.sunk | while | flops 2079339520 | bytes 211768528 | solution.py:185
  354.5 20.0 %bitcast_dynamic-update-slice_fusion.10 = bf16[2,512,12,64]{1,3,2,0:T(8,128)(2,1)} fusion(bf16[2,512,12,64]{1,3,2,0:T(8,128)(2,1)} %get-tuple-element.442, s32[]{:T(128)S(6)} %copy.158, f32[12,512,512]{1,2,0:T(8,128)} %fusion.195, f32[12,512,512]{1,2,0:T(8,128)} %copy-done.2, f32[12,512]{1,0:T(8,128)S(1)} %dynamic-slice_bitcast_fusion.2, ...), kind=kOutput, calls=%fused_computation.35.clone.1 | convolution fusion | flops 430971392 | bytes 52757504 | tf_op jit(solution)/shard_map/while/body/eval_jaxpr/hqk,qhe->khe/dot_general | solution.py:70
  374.4 19.8 %bitcast_dynamic-update-slice_fusion.9 = f32[2,512,12,64]{1,3,2,0:T(8,128)} fusion(f32[2,512,12,64]{1,3,2,0:T(8,128)} %get-tuple-element.441, s32[]{:T(128)S(6)} %copy.158, f32[12,512,512]{1,2,0:T(8,128)} %fusion.195, f32[12,512,512]{1,2,0:T(8,128)} %copy-done.2, f32[12,512]{1,0:T(8,128)S(1)} %dynamic-slice_bitcast_fusion.2, ...), kind=kOutput, calls=%fused_computation.36.clone.1 | convolution fusion | flops 430971392 | bytes 52757504 | tf_op jit(solution)/shard_map/while/body/eval_jaxpr/hqk,khe->qhe/dot_general | solution.py:69
  407.8 19.6 %bitcast_dynamic-update-slice_fusion.10 = bf16[2,512,12,64]{1,3,2,0:T(8,128)(2,1)} fusion(bf16[2,512,12,64]{1,3,2,0:T(8,128)(2,1)} %get-tuple-element.442, s32[]{:T(128)S(6)} %copy.158, f32[12,512,512]{1,2,0:T(8,128)} %fusion.195, f32[12,512,512]{1,2,0:T(8,128)} %copy-done.2, f32[12,512]{1,0:T(8,128)S(1)} %dynamic-slice_bitcast_fusion.2, ...), kind=kOutput, calls=%fused_computation.35.clone.1 | convolution fusion | flops 430971392 | bytes 52757504 | tf_op jit(solution)/shard_map/while/body/eval_jaxpr/hqk,qhe->khe/dot_general | solution.py:70
  427.4 19.6 %bitcast_dynamic-update-slice_fusion.9 = f32[2,512,12,64]{1,3,2,0:T(8,128)} fusion(f32[2,512,12,64]{1,3,2,0:T(8,128)} %get-tuple-element.441, s32[]{:T(128)S(6)} %copy.158, f32[12,512,512]{1,2,0:T(8,128)} %fusion.195, f32[12,512,512]{1,2,0:T(8,128)} %copy-done.2, f32[12,512]{1,0:T(8,128)S(1)} %dynamic-slice_bitcast_fusion.2, ...), kind=kOutput, calls=%fused_computation.36.clone.1 | convolution fusion | flops 430971392 | bytes 52757504 | tf_op jit(solution)/shard_map/while/body/eval_jaxpr/hqk,khe->qhe/dot_general | solution.py:69
  467.5 9.8 convolution_bitcast_fusion.1
  477.2 11.0 copy.123
  498.3 10.6 fusion.80
  510.9 10.3 fusion.104
  524.8 98.9 %reduce-scatter.16.cloned.1.call-done = f32[96,2304]{1,0:T(8,128)} async-done(((f32[768,2304]{1,0:T(8,128)}), f32[96,2304]{1,0:T(8,128)}) %reduce-scatter.16.cloned.1.call-update) | async-done | bytes 884752
  626.9 163.5 %reduce-scatter.12.cloned.1.call-done = f32[96,3072]{1,0:T(8,128)} async-done(((f32[768,3072]{1,0:T(8,128)}), f32[96,3072]{1,0:T(8,128)}) %reduce-scatter.12.cloned.1.call-update) | async-done | bytes 1179664 | tf_op jit(solution)/shard_map/reduce_scatter | solution.py:170
  792.5 164.4 %reduce-scatter.14.cloned.1.call-done = f32[3072,96]{0,1:T(8,128)} async-done(((f32[3072,768]{0,1:T(8,128)}), f32[3072,96]{0,1:T(8,128)}) %reduce-scatter.14.cloned.1.call-update) | async-done | bytes 1179664 | tf_op jit(solution)/shard_map/reduce_scatter | solution.py:171
  963.7 35.2 %all-reduce = bf16[3072]{0:T(1024)(128)(2,1)S(1)} all-reduce(f32[3072]{0:T(1024)S(1)} %copy-done.48), channel_id=7, replica_groups=mesh['wide'=8,'narrow'=4] {'wide'}, use_global_device_ids=true, to_apply=%region_39.40.clone | all-reduce | flops 3072 | bytes 18432
  998.9 22.7 %reduce-scatter.18.cloned.1.call-done = f32[96,8]{1,0:T(8,128)} async-done(((f32[768,8]{1,0:T(8,128)}), f32[96,8]{1,0:T(8,128)}) %reduce-scatter.18.cloned.1.call-update) | async-done | bytes 3088
  1029.3 44.3 %all-reduce.5.cloned.1.call-done = (bf16[3,96,768]{1,2,0:T(8,128)(2,1)}, bf16[768,96]{0,1:T(8,128)(2,1)}, bf16[96,3072]{1,0:T(8,128)(2,1)}, bf16[3072,96]{0,1:T(8,128)(2,1)}) async-done(((bf16[3,96,768]{1,2,0:T(8,128)(2,1)}, bf16[768,96]{0,1:T(8,128)(2,1)}, bf16[96,3072]{1,0:T(8,128)(2,1)}, bf16[3072,96]{0,1:T(8,128)(2,1)}), (bf16[3,96,768]{1,2,0:T(8,128)(2,1)}, bf16[768,96]{0,1:T(8,128)(2,1)}, ...) | async-done | bytes 1769488 | tf_op jit(solution)/shard_map/psum | solution.py:216
  1085.1 9.9 bitcast_add_fusion
  1095.0 21.8 %psum.55 = f32[]{:T(128)} all-reduce(f32[]{:T(128)S(6)} %add.292), channel_id=1, replica_groups=mesh['wide'=8,'narrow'=4] {'wide'}, use_global_device_ids=true, to_apply=%region_42.43 | all-reduce | flops 1 | bytes 8 | tf_op jit(solution)/shard_map/psum | solution.py:231
  (275 shorter events, 224.1 us)
Async XLA Ops:
  7.2 61.3 %copy-start = (bf16[2,76,768]{2,0,1:T(2,128)(2,1)S(1)}, bf16[2,76,768]{2,0,1:T(2,128)(2,1)}, u32[]{:S(2)}) copy-start(bf16[2,76,768]{2,0,1:T(2,128)(2,1)} %param.29) | copy-start | bytes 700420
  7.2 71.9 %all-gather.7.cloned.1.call-start = ((), (), s32[]{:S(2)}) async-start(), calls=%async_computation.5 | async-start | bytes 3981312 | tf_op jit(solution)/shard_map/all_gather | solution.py:114
  9.4 59.1 %copy-start.58 = (s32[2,76]{1,0:T(2,128)S(1)}, s32[2,76]{1,0:T(2,128)}, u32[]{:S(2)}) copy-start(s32[2,76]{1,0:T(2,128)} %param.27) | copy-start | bytes 1828
  9.4 117.9 %all-gather.9.cloned.1.call-start = ((), (), s32[]{:S(2)}) async-start(), calls=%async_computation.6 | async-start | bytes 1327104 | tf_op jit(solution)/shard_map/all_gather | solution.py:115
  11.2 191.8 %all-gather.11.cloned.1.call-start = ((), (), s32[]{:S(2)}) async-start(), calls=%async_computation.7 | async-start | bytes 5308416 | tf_op jit(solution)/shard_map/all_gather | solution.py:119
  12.1 271.5 %all-gather.13.cloned.1.call-start = ((), (), s32[]{:S(2)}) async-start(), calls=%async_computation.8 | async-start | bytes 5308416 | tf_op jit(solution)/shard_map/all_gather | solution.py:120
  13.1 510.1 %reduce-scatter.10.cloned.1.call-start = ((), (), s32[]{:S(2)}) async-start(), calls=%async_computation.9 | async-start | bytes 2654208 | tf_op jit(solution)/shard_map/reduce_scatter | solution.py:212
  68.4 17.3 %copy-start.38 = (f32[768]{0:T(1024)}, f32[768]{0:T(1024)S(1)}, u32[]{:S(2)}) copy-start(f32[768]{0:T(1024)S(1)} %get-tuple-element.224) | copy-start | bytes 9220
  68.4 215.2 %copy-start.36 = (f32[768]{0:T(1024)}, f32[768]{0:T(1024)S(1)}, u32[]{:S(2)}) copy-start(f32[768]{0:T(1024)S(1)} %get-tuple-element.227) | copy-start | bytes 9220
  68.4 251.5 %copy-start.34 = (f32[768]{0:T(1024)}, f32[768]{0:T(1024)S(1)}, u32[]{:S(2)}) copy-start(f32[768]{0:T(1024)S(1)} %get-tuple-element.228) | copy-start | bytes 9220
  131.2 188.7 %copy-start.30 = (f32[1024]{0:T(1024)}, f32[1024]{0:T(1024)S(1)}, u32[]{:S(2)}) copy-start(f32[1024]{0:T(1024)S(1)} %broadcast_multiply_fusion.4) | copy-start | bytes 12292
  133.4 186.6 %copy-start.32 = (f32[1024]{0:T(1024)}, f32[1024]{0:T(1024)S(1)}, u32[]{:S(2)}) copy-start(f32[1024]{0:T(1024)S(1)} %add_rsqrt_fusion.1) | copy-start | bytes 12292
  202.9 80.7 %copy-start.51 = (f32[768]{0:T(1024)S(1)}, f32[768]{0:T(1024)}, u32[]{:S(2)}) copy-start(f32[768]{0:T(1024)} %get-tuple-element.226) | copy-start | bytes 9220
  296.6 16.9 %slice-start = ((s8[4718592]{0:T(1024)(128)(4,1)}), s8[4194304]{0:T(1024)(128)(4,1)S(1)}, s32[]{:S(2)}) async-start(s8[4718592]{0:T(1024)(128)(4,1)} %bitcast.173), calls=%async_computation.15 | async-start | bytes 8388608
  299.7 13.8 %copy-start.5 = (f32[1024,768]{1,0:T(8,128)S(1)}, f32[1024,768]{1,0:T(8,128)}, u32[]{:S(2)}) copy-start(f32[1024,768]{1,0:T(8,128)} %copy-done.4) | copy-start | bytes 9437188
  299.7 13.8 %slice-start.1 = ((s8[4718592]{0:T(1024)(128)(4,1)}), s8[524288]{0:T(1024)(128)(4,1)S(1)}, s32[]{:S(2)}) async-start(s8[4718592]{0:T(1024)(128)(4,1)} %bitcast.173), calls=%async_computation.16 | async-start | bytes 1048576
  340.3 283.5 %reduce-scatter.16.cloned.1.call-start = ((), (), s32[]{:S(2)}) async-start(), calls=%async_computation.12 | async-start | bytes 7962624
  496.4 293.9 %reduce-scatter.12.cloned.1.call-start = ((), (), s32[]{:S(2)}) async-start(), calls=%async_computation.10 | async-start | bytes 10616832 | tf_op jit(solution)/shard_map/reduce_scatter | solution.py:170
  509.0 447.9 %reduce-scatter.14.cloned.1.call-start = ((), (), s32[]{:S(2)}) async-start(), calls=%async_computation.11 | async-start | bytes 10616832 | tf_op jit(solution)/shard_map/reduce_scatter | solution.py:171
  521.3 500.4 %reduce-scatter.18.cloned.1.call-start = ((), (), s32[]{:S(2)}) async-start(), calls=%async_computation.13 | async-start | bytes 442368
  523.1 550.5 %all-reduce.5.cloned.1.call-start = ((), (), s32[]{:S(2)}) async-start(), calls=%async_computation.14 | async-start | bytes 3833856 | tf_op jit(solution)/shard_map/psum | solution.py:216
  625.6 333.5 %copy-start.16 = (f32[3,96,768]{2,1,0:T(8,128)S(1)}, f32[3,96,768]{2,1,0:T(8,128)}, u32[]{:S(2)}) copy-start(f32[3,96,768]{2,1,0:T(8,128)} %param.30) | copy-start | bytes 2654212
  792.5 167.0 %copy-start.28 = (f32[3,96,768]{2,1,0:T(8,128)S(1)}, f32[3,96,768]{2,1,0:T(8,128)}, u32[]{:S(2)}) copy-start(f32[3,96,768]{2,1,0:T(8,128)} %param.31) | copy-start | bytes 2654212
  1085.1 32.5 %copy-start.22 = (bf16[3,96,768]{1,2,0:T(8,128)(2,1)S(1)}, bf16[3,96,768]{1,2,0:T(8,128)(2,1)}, u32[]{:S(2)}) copy-start(bf16[3,96,768]{1,2,0:T(8,128)(2,1)} %get-tuple-element.264) | copy-start | bytes 1327108
  (53 other events, 218.7 us)
Sparse Core Ops, SparseCore 0:
  10.8 68.2 all-gather.6
  81.9 39.5 all-gather.8
  124.2 78.6 all-gather.10
  205.5 78.0 all-gather.12
  340.4 67.1 reduce-scatter.9
  496.6 127.1 reduce-scatter.15
  627.8 162.4 reduce-scatter.11
  794.3 162.5 reduce-scatter.13
  961.1 60.4 reduce-scatter.17
  1025.4 48.2 all-reduce.4
where the time goes:
time: 1150 us
  waiting for transfers between devices  639 us (56%)
  matrix products  217 us (19%)
  blocking collectives  117 us (10%)
  local copies, waits for them, and re-layouts  93.8 us (8%)
  other arithmetic  57.3 us (5%)
  between operations  21.7 us (2%)
    reduce_scatter x1, waiting for transfers between devices, shards(): lax.psum_scatter(ddown, 'wide', scatter_dimension=1, tiled=True)  164 us
    reduce_scatter x1, waiting for transfers between devices, shards(): lax.psum_scatter(dup, 'wide', scatter_dimension=0, tiled=True)  163 us
    unnamed x12, waiting for transfers between devices  122 us
    all_gather x1, waiting for transfers between devices, shards(): lax.all_gather(up_weight.astype(jnp.bfloat16), 'wide', axis=0, tiled=True)  69.5 us
    all_gather x1, waiting for transfers between devices, shards(): lax.all_gather(down_weight.astype(jnp.bfloat16), 'wide', axis=1, tiled=True)  68 us
    unnamed x135, local copies, waits for them, and re-layouts  45.8 us
    psum x1, waiting for transfers between devices, shards(): lax.psum(own_qkv.astype(jnp.bfloat16), 'narrow').astype(jnp.float32)  44.3 us
    dot_general x2, matrix products, attend_back(): jnp.einsum('hqk,qhe->khe', dscore, query, preferred_element_type=jnp.floa...  39.6 us
  transfers between devices with their start and end apart: 10, of which 8 were waited for; matrix products, arithmetic and copies ran while one was open for 23% of the time, Pallas kernels for 0%

commit v1 on v0

v1 whole, which is shorter than its diff:
```python
import functools

import jax
import jax.numpy as jnp
from jax import lax
from jax.experimental import pallas as pl
from jax.experimental.pallas import tpu as pltpu
from jax.sharding import PartitionSpec as P

HEADS = 12
HEAD_DIM = 64
STEP = 10

LN_EPS = 1e-06
SQRT_HALF = 0.7071067811865476
INV_ROOT_TWO_PI = 0.3989422804014327
CLIP_LIMIT = 1.0
BETA_ONE = 0.9
BETA_TWO = 0.999
LEARN_RATE = 0.05
OUTPUT_RATE = 0.2
VECTOR_RATE = 0.5
BIAS_RATE = 0.3
DECAY_RATE = 0.01
ADAM_EPS = 1e-08

MESH = pl.DeviceIdType.MESH


def when(cond, body):
    if cond is None:
        body()
    else:
        pl.when(cond)(body)


class Sends:
    def __init__(self):
        self.started = []

    def start(self, cond, make):
        when(cond, lambda: make().start())
        self.started.append((cond, make))

    def finish(self):
        for cond, make in self.started:
            when(cond, lambda make=make: make().wait_send())


def both(a, b):
    return b if a is None else (a if b is None else jnp.logical_and(a, b))


def place():
    w, n = lax.axis_index("wide"), lax.axis_index("narrow")
    return w // 2, lax.rem(w, 2), n // 2, lax.rem(n, 2)


def flip(v):
    return 1 - v


def dev(z, y, x, c):
    return (z * 2 + y, x * 2 + c)


def meet(z, y, x, c, diagonal):
    bar = pltpu.get_barrier_semaphore()
    peers = [(None, dev(z, flip(y), x, c)), (None, dev(z, y, flip(x), c)), (None, dev(z, y, x, flip(c)))]
    if diagonal:
        peers.append((None, dev(z, y, flip(x), flip(c))))
    peers += [(z > 0, dev(z - 1, y, x, c)), (z < 3, dev(z + 1, y, x, c))]
    for cond, peer in peers:
        when(cond, lambda peer=peer: pl.semaphore_signal(bar, inc=1, device_id=peer, device_id_type=MESH))
    inner = jnp.logical_and(z > 0, z < 3)
    count = 4 if diagonal else 3
    pl.semaphore_wait(bar, count + 1 + jnp.where(inner, 1, 0))


def gather_kernel(rows, cols, attn, up, down, small, attn_full, up_full, down_full, small_full, send_sem, recv_sem, small_send, small_recv, own_sem):
    z, y, x, c = place()
    edge = x == c
    third = cols // 3
    mine, across = x + c, 2 * flip(x)
    fulls = (attn_full, up_full, down_full)
    shards = (attn, up, down)
    sends = Sends()
    zl, zh = z > 0, z < 3

    def spot(p, zz, yy, t):
        return fulls[p].at[pl.ds(pl.multiple_of((zz * 2 + yy) * rows, rows), rows), pl.ds(pl.multiple_of(t * third, third), third)]

    def push(cond, p, zz, yy, t, kind, to, src=None):
        def make():
            w = zz * 2 + yy
            where = spot(p, zz, yy, t)
            return pltpu.make_async_remote_copy(
                src_ref=where if src is None else src,
                dst_ref=where,
                send_sem=send_sem.at[kind, p, w],
                recv_sem=recv_sem.at[p, w, t],
                device_id=to,
                device_id_type=MESH,
            )

        sends.start(cond, make)

    def small_push(cond, zz, yy, kind, to, src=None):
        def make():
            w = zz * 2 + yy
            where = small_full.at[w]
            return pltpu.make_async_remote_copy(
                src_ref=where if src is None else src,
                dst_ref=where,
                send_sem=small_send.at[kind, w],
                recv_sem=small_recv.at[w],
                device_id=to,
                device_id_type=MESH,
            )

        sends.start(cond, make)

    def arrive(cond, p, zz, yy, t):
        def body():
            where = spot(p, zz, yy, t)
            w = zz * 2 + yy
            pltpu.make_async_remote_copy(where, where, send_sem.at[0, p, w], recv_sem.at[p, w, t], dev(z, y, x, c), device_id_type=MESH).wait_recv()

        when(cond, body)

    def small_arrive(cond, zz, yy):
        def body():
            w = zz * 2 + yy
            pltpu.make_async_remote_copy(small_full.at[w], small_full.at[w], small_send.at[0, w], small_recv.at[w], dev(z, y, x, c), device_id_type=MESH).wait_recv()

        when(cond, body)

    UP, DOWN, SIDE, OVER, NEAR, PASS = range(6)
    above, below, beside = dev(z + 1, y, x, c), dev(z - 1, y, x, c), dev(z, flip(y), x, c)
    over, near = dev(z, y, flip(x), c), dev(z, y, x, flip(c))

    def own(p):
        src = shards[p].at[:, pl.ds(pl.multiple_of(mine * third, third), third)]
        push(zh, p, z, y, mine, UP, above, src)
        push(zl, p, z, y, mine, DOWN, below, src)
        push(None, p, z, y, mine, SIDE, beside, src)

    def z_step(p, d):
        for cond, zz, onward, kind, to in ((z - d >= 0, z - d, zh, UP, above), (z + d <= 3, z + d, zl, DOWN, below)):
            arrive(cond, p, zz, y, mine)
            push(both(cond, onward), p, zz, y, mine, kind, to)
            push(cond, p, zz, y, mine, SIDE, beside)
            push(both(cond, edge), p, zz, y, mine, OVER, over)
            push(cond, p, zz, y, mine, NEAR, near)

    def y_step(p, d):
        steps = ((None, z),) if d == 0 else ((z - d >= 0, z - d), (z + d <= 3, z + d))
        for cond, zz in steps:
            arrive(cond, p, zz, flip(y), mine)
            push(both(cond, edge), p, zz, flip(y), mine, OVER, over)
            push(cond, p, zz, flip(y), mine, NEAR, near)

    def x_step(p, d):
        mid = jnp.logical_not(edge)
        for yy in (y, flip(y)):
            if d == 0:
                steps = () if yy is y else ((None, z),)
            else:
                steps = ((z - d >= 0, z - d), (z + d <= 3, z + d))
            for cond, zz in steps:
                cond = both(cond, mid)
                arrive(cond, p, zz, yy, across)
                push(cond, p, zz, yy, across, PASS, near)

    def last(p, d):
        for yy in (y, flip(y)):
            if d == 0:
                steps = () if yy is y else ((None, z),)
            else:
                steps = ((z - d >= 0, z - d), (z + d <= 3, z + d))
            for cond, zz in steps:
                arrive(cond, p, zz, yy, x + flip(c))
                arrive(both(cond, edge), p, zz, yy, across)

    def small_z(d):
        for cond, zz, onward, kind, to in ((z - d >= 0, z - d, zh, UP, above), (z + d <= 3, z + d, zl, DOWN, below)):
            small_arrive(cond, zz, y)
            small_push(both(cond, onward), zz, y, kind, to)
            small_push(cond, zz, y, SIDE, beside)

    meet(z, y, x, c, False)
    small_push(zh, z, y, UP, above, small)
    small_push(zl, z, y, DOWN, below, small)
    small_push(None, z, y, SIDE, beside, small)
    own(0)
    w = z * 2 + y
    copies = []
    for p in range(3):
        copies.append(pltpu.make_async_copy(shards[p], fulls[p].at[pl.ds(pl.multiple_of(w * rows, rows), rows)], own_sem.at[p]))
    copies.append(pltpu.make_async_copy(small, small_full.at[w], own_sem.at[3]))
    for copy in copies:
        copy.start()
    for d in range(1, 4):
        small_z(d)
    order = [
        lambda: z_step(0, 1), lambda: own(1), lambda: y_step(0, 0), lambda: z_step(0, 2), lambda: y_step(0, 1), lambda: x_step(0, 0), lambda: z_step(0, 3),
        lambda: y_step(0, 2), lambda: x_step(0, 1), lambda: z_step(1, 1), lambda: own(2), lambda: y_step(0, 3), lambda: x_step(0, 2), lambda: z_step(1, 2), lambda: y_step(1, 0), lambda: x_step(0, 3), lambda: z_step(1, 3),
        lambda: y_step(1, 1), lambda: x_step(1, 0), lambda: z_step(2, 1), lambda: y_step(1, 2), lambda: x_step(1, 1), lambda: z_step(2, 2), lambda: y_step(1, 3), lambda: x_step(1, 2), lambda: z_step(2, 3),
        lambda: y_step(2, 0), lambda: x_step(1, 3), lambda: y_step(2, 1), lambda: x_step(2, 0), lambda: y_step(2, 2), lambda: x_step(2, 1), lambda: y_step(2, 3), lambda: x_step(2, 2), lambda: x_step(2, 3),
    ]
    for step in order:
        step()
    for d in range(4):
        for cond, zz in (((None, z),) if d == 0 else ((z - d >= 0, z - d), (z + d <= 3, z + d))):
            small_arrive(cond, zz, flip(y))
    for p in range(3):
        for d in range(4):
            last(p, d)
    sends.finish()
    for copy in copies:
        copy.wait()


def gather(attn, up, down, small):
    rows, cols = attn.shape
    full = jax.ShapeDtypeStruct((8 * rows, cols), attn.dtype)
    anywhere = pl.BlockSpec(memory_space=pl.ANY)
    return pl.pallas_call(
        functools.partial(gather_kernel, rows, cols),
        out_shape=(full, full, full, jax.ShapeDtypeStruct((8,) + small.shape, small.dtype)),
        in_specs=[anywhere] * 4,
        out_specs=(anywhere,) * 4,
        scratch_shapes=[
            pltpu.SemaphoreType.DMA((6, 3, 8)),
            pltpu.SemaphoreType.DMA((3, 8, 3)),
            pltpu.SemaphoreType.DMA((3, 8)),
            pltpu.SemaphoreType.DMA((8,)),
            pltpu.SemaphoreType.DMA((4,)),
        ],
        compiler_params=pltpu.CompilerParams(collective_id=0, has_side_effects=True),
    )(attn, up, down, small)


E = 768
M = 1536
SLAB = 32
ORDER = (3, 0, 2, 1)


def slabs(rows, body):
    @pl.loop(0, rows // SLAB)
    def _(i):
        body(pl.ds(pl.multiple_of(i * SLAB, SLAB), SLAB))


def f32(v):
    return v.astype(jnp.float32)


def reduce_kernel(rows, g_a, g_b, g_c, small, out, small_out, sib, xs, xr, acc, yr, zu, zd, mr,
                  sib_s, sib_r, x_s, x_r, y_s, y_r, z_s, z_r, m_s, m_r, f_s, f_r,
                  ssib, sx, sy, szu, szd, sacc, sm_s, sm_r, phases=3):
    z, y, x, c = place()
    edge = x == c
    mid = jnp.logical_not(edge)
    grads = (g_a, g_b, g_c)
    sends = Sends()
    me = dev(z, y, x, c)
    above, below, beside = dev(z + 1, y, x, c), dev(z - 1, y, x, c), dev(z, flip(y), x, c)
    over, near, diag = dev(z, y, flip(x), c), dev(z, y, x, flip(c)), dev(z, y, flip(x), flip(c))
    ecol = pl.multiple_of(x * 2304, 768)
    pair = rows * 2

    def zrows(zz):
        return pl.ds(zz * pair, pair)

    def wrows(zz, yy):
        return pl.ds(pl.multiple_of((zz * 2 + yy) * rows, rows), rows)

    def copy(src, dst, ss, rs, to):
        return pltpu.make_async_remote_copy(src_ref=src, dst_ref=dst, send_sem=ss, recv_sem=rs, device_id=to, device_id_type=MESH)

    def wait(cond, dst, rs):
        when(cond, lambda: copy(dst, dst, rs, rs, me).wait_recv())

    meet(z, y, x, c, True)

    for p in range(phases):
        for zz in ORDER:
            sends.start(edge, lambda p=p, zz=zz: copy(
                grads[p].at[zrows(zz), pl.ds(pl.multiple_of(768 * flip(x), 768), 2304)], sib.at[p, zrows(zz)], sib_s.at[p, zz], sib_r.at[p, zz], near))
            sends.start(mid, lambda p=p, zz=zz: copy(
                grads[p].at[zrows(zz), pl.ds(ecol, E)], sib.at[p, zrows(zz), pl.ds(0, E)], sib_s.at[p, zz], sib_r.at[p, zz], near))

    sends.start(None, lambda: copy(small, ssib, sm_s.at[0], sm_r.at[0], near))
    wait(None, ssib, sm_r.at[0])
    sacc[...] = small[...] + ssib[...]
    sends.start(None, lambda: copy(sacc, sx, sm_s.at[1], sm_r.at[1], over))

    moff = 768 * x
    ooff = 1536 * flip(x)

    def first(p, zz):
        @pl.when(mid)
        def _():
            wait(None, sib.at[p, zrows(zz)], sib_r.at[p, zz])

            def one(r):
                r = pl.ds(zz * pair + r.start, SLAB)
                xs[p, r, :] = (f32(grads[p][r, pl.ds(pl.multiple_of(2304 * flip(x), 768), E)]) + f32(sib[p, r, pl.ds(pl.multiple_of(ooff, 768), E)])).astype(jnp.bfloat16)
                acc[p, r, :] = (f32(grads[p][r, pl.ds(768, M)]) + f32(sib[p, r, pl.ds(pl.multiple_of(moff, 768), M)])).astype(jnp.bfloat16)

            slabs(pair, one)

        sends.start(mid, lambda: copy(xs.at[p, zrows(zz)], xr.at[p, zrows(zz)], x_s.at[p, zz], x_r.at[p, zz], over))

        @pl.when(edge)
        def _():
            wait(None, sib.at[p, zrows(zz), pl.ds(0, E)], sib_r.at[p, zz])
            wait(None, xr.at[p, zrows(zz)], x_r.at[p, zz])

            def one(r):
                r = pl.ds(zz * pair + r.start, SLAB)
                acc[p, r, pl.ds(0, E)] = (f32(grads[p][r, pl.ds(ecol, E)]) + f32(sib[p, r, pl.ds(0, E)]) + f32(xr[p, r, :])).astype(jnp.bfloat16)

            slabs(pair, one)

        for cond, width in ((edge, E), (mid, M)):
            sends.start(cond, lambda width=width: copy(
                acc.at[p, wrows(zz, flip(y)), pl.ds(0, width)], yr.at[p, zz, :, pl.ds(0, width)], y_s.at[p, zz], y_r.at[p, zz], beside))

    def add_into(cond, p, zz, buffer, sem):
        for role, width in ((edge, E), (mid, M)):
            @pl.when(both(cond, role))
            def _():
                wait(None, buffer.at[p, zz, :, pl.ds(0, width)], sem)
                base = (zz * 2 + y) * rows

                def one(r):
                    here = pl.ds(pl.multiple_of(base + r.start, SLAB), SLAB)
                    acc[p, here, pl.ds(0, width)] = (f32(acc[p, here, pl.ds(0, width)]) + f32(buffer[p, zz, r, pl.ds(0, width)])).astype(jnp.bfloat16)

                slabs(rows, one)

    def z_push(cond, p, zz, buffer, k, to):
        for role, width in ((edge, E), (mid, M)):
            sends.start(both(cond, role), lambda width=width: copy(
                acc.at[p, wrows(zz, y), pl.ds(0, width)], buffer.at[p, zz, :, pl.ds(0, width)], z_s.at[k, p, zz], z_r.at[k, p, zz], to))

    def second(p, zz):
        add_into(None, p, zz, yr, y_r.at[p, zz])

    def line(p, t):
        up = both(z <= t, z < 3)
        zz = jnp.where(up, 3 + z - t, 0)
        add_into(both(up, z > 0), p, zz, zu, z_r.at[0, p, zz])
        z_push(up, p, zz, zu, 0, above)
        down = both(3 - z <= t, z > 0)
        zz = jnp.where(down, z + t - 3, 0)
        add_into(both(down, z < 3), p, zz, zd, z_r.at[1, p, zz])
        z_push(down, p, zz, zd, 1, below)

    def owner(p):
        add_into(z > 0, p, z, zu, z_r.at[0, p, z])
        add_into(z < 3, p, z, zd, z_r.at[1, p, z])

    def third(p):
        mine = wrows(z, y)
        sends.start(mid, lambda: copy(acc.at[p, mine], mr.at[p], m_s.at[p], m_r.at[p], diag))

        @pl.when(edge)
        def _():
            base = (z * 2 + y) * rows

            def one(r):
                here = pl.ds(pl.multiple_of(base + r.start, SLAB), SLAB)
                out[p, r, pl.ds(ecol, E)] = acc[p, here, pl.ds(0, E)]

            slabs(rows, one)

        for k, to in enumerate((near, over, diag)):
            sends.start(edge, lambda k=k, to=to: copy(
                out.at[p, :, pl.ds(ecol, E)], out.at[p, :, pl.ds(ecol, E)], f_s.at[p, k], f_r.at[p, x], to))

        @pl.when(mid)
        def _():
            wait(None, mr.at[p], m_r.at[p])
            base = (z * 2 + y) * rows

            def one(r):
                here = pl.ds(pl.multiple_of(base + r.start, SLAB), SLAB)
                out[p, r, pl.ds(E, M)] = (f32(acc[p, here, :]) + f32(mr[p, r, :])).astype(jnp.bfloat16)

            slabs(rows, one)

        sends.start(mid, lambda: copy(out.at[p, :, pl.ds(E, M)], out.at[p, :, pl.ds(E, M)], f_s.at[p, 0], f_r.at[p, 2], near))

    def last(p):
        for xx in range(2):
            wait(jnp.logical_not(both(edge, x == xx)), out.at[p, :, pl.ds(2304 * xx, E)], f_r.at[p, xx])
        wait(edge, out.at[p, :, pl.ds(E, M)], f_r.at[p, 2])

    def small_rest():
        wait(None, sx, sm_r.at[1])
        ssib[...] = sacc[...] + sx[...]

    def small_y():
        small_rest()
        for zz in range(4):
            sends.start(None, lambda zz=zz: copy(ssib.at[zz * 2 + flip(y)], sy.at[zz], sm_s.at[2 + zz], sm_r.at[2 + zz], beside))

    def small_add():
        for zz in range(4):
            wait(None, sy.at[zz], sm_r.at[2 + zz])
            sy[zz] = sy[zz] + ssib[zz * 2 + y]

    def small_line():
        for zz in ORDER:
            @pl.when(both(z <= zz, z > 0))
            def _():
                wait(None, szu.at[zz], sm_r.at[6 + zz])
                sy[zz] = sy[zz] + szu[zz]
            sends.start(z < zz, lambda zz=zz: copy(sy.at[zz], szu.at[zz], sm_s.at[6 + zz], sm_r.at[6 + zz], above))

            @pl.when(both(z >= zz, z < 3))
            def _():
                wait(None, szd.at[zz], sm_r.at[10 + zz])
                sy[zz] = sy[zz] + szd[zz]
            sends.start(z > zz, lambda zz=zz: copy(sy.at[zz], szd.at[zz], sm_s.at[10 + zz], sm_r.at[10 + zz], below))

    def F(p):
        for zz in ORDER:
            first(p, zz)

    def S(p):
        for zz in ORDER:
            second(p, zz)

    def L(p):
        for t in range(3):
            line(p, t)
        owner(p)

    F(0)
    small_y()
    F(1)
    S(0)
    small_add()
    F(2)
    L(0)
    small_line()
    S(1)
    L(1)
    third(0)
    S(2)
    L(2)
    third(1)
    third(2)
    small_out[...] = sy[z]
    for p in range(phases):
        last(p)
    sends.finish()


def reduce(g_a, g_b, g_c, small):
    total, cols = g_a.shape
    rows = total // 8
    b = jnp.bfloat16
    f = jnp.float32
    dma = pltpu.SemaphoreType.DMA
    vm = pl.BlockSpec(memory_space=pltpu.VMEM)
    one = small.shape[1:]
    return pl.pallas_call(
        functools.partial(reduce_kernel, rows),
        out_shape=(jax.ShapeDtypeStruct((3, rows, cols), b), jax.ShapeDtypeStruct(one, f)),
        in_specs=[vm] * 4,
        out_specs=(vm, vm),
        scratch_shapes=[
            pltpu.VMEM((3, total, 2304), b),
            pltpu.VMEM((3, total, E), b),
            pltpu.VMEM((3, total, E), b),
            pltpu.VMEM((3, total, M), b),
            pltpu.VMEM((3, 4, rows, M), b),
            pltpu.VMEM((3, 4, rows, M), b),
            pltpu.VMEM((3, 4, rows, M), b),
            pltpu.VMEM((3, rows, M), b),
            dma((3, 4)), dma((3, 4)), dma((3, 4)), dma((3, 4)), dma((3, 4)), dma((3, 4)),
            dma((2, 3, 4)), dma((2, 3, 4)), dma((3,)), dma((3,)), dma((3, 3)), dma((3, 3)),
            pltpu.VMEM((8,) + one, f), pltpu.VMEM((8,) + one, f),
            pltpu.VMEM((4,) + one, f), pltpu.VMEM((4,) + one, f), pltpu.VMEM((4,) + one, f),
            pltpu.VMEM((8,) + one, f),
            dma((14,)), dma((14,)),
        ],
        compiler_params=pltpu.CompilerParams(collective_id=1, has_side_effects=True, vmem_limit_bytes=60 * 2**20),
    )(g_a, g_b, g_c, small)


def layer_norm(values, gain, shift):
    center = values - jnp.mean(values, axis=-1, keepdims=True)
    inverse = lax.rsqrt(jnp.mean(center * center, axis=-1, keepdims=True) + LN_EPS)
    normed = center * inverse
    return (normed * gain + shift, normed, inverse)


def norm_back(incoming, normed, inverse, gain):
    dgain = jnp.sum(incoming * normed, axis=0)
    dshift = jnp.sum(incoming, axis=0)
    scaled = incoming * gain
    dvalues = inverse * (
        scaled
        - jnp.mean(scaled, axis=-1, keepdims=True)
        - normed * jnp.mean(scaled * normed, axis=-1, keepdims=True)
    )
    return (dvalues, dgain, dshift)


def mm(a, b, dims, out=jnp.float32):
    return lax.dot_general(a, b, (dims, ((), ())), preferred_element_type=jnp.float32).astype(out)


NN = ((1,), (0,))
NT = ((1,), (1,))
TN = ((0,), (0,))


def split_heads(values, seqs, length):
    return values.reshape(seqs, length, HEADS, HEAD_DIM)


def attend(pieces):
    query, key, value = pieces
    raw = jnp.einsum("qhe,khe->hqk", query, key, preferred_element_type=jnp.float32) * HEAD_DIM ** (
        -0.5
    )
    peak = jnp.max(raw, axis=-1, keepdims=True)
    expo = jnp.exp(raw - peak)
    total = jnp.sum(expo, axis=-1, keepdims=True)
    probs = (expo / total).astype(jnp.bfloat16)
    mixed = jnp.einsum("hqk,khe->qhe", probs, value, preferred_element_type=jnp.float32)
    return mixed.astype(jnp.bfloat16)


def attend_back(pieces):
    query, key, value, dmixed = pieces
    scale = HEAD_DIM ** (-0.5)
    raw = jnp.einsum("qhe,khe->hqk", query, key, preferred_element_type=jnp.float32) * scale
    probs = jax.nn.softmax(raw, axis=-1)
    dprobs = jnp.einsum("qhe,khe->hqk", dmixed, value, preferred_element_type=jnp.float32)
    dscore = probs * (dprobs - jnp.sum(dprobs * probs, axis=-1, keepdims=True))
    dscore = (dscore * scale).astype(jnp.bfloat16)
    dquery = jnp.einsum("hqk,khe->qhe", dscore, key, preferred_element_type=jnp.float32)
    dkey = jnp.einsum("hqk,qhe->khe", dscore, query, preferred_element_type=jnp.float32)
    dvalue = jnp.einsum(
        "hqk,qhe->khe", probs.astype(jnp.bfloat16), dmixed, preferred_element_type=jnp.float32
    )
    return (dquery, dkey, dvalue)


def adam_step(weight, first, second, grad, factor, decay, rate):
    grad = grad * factor
    first_new = BETA_ONE * first + (1.0 - BETA_ONE) * grad
    second_new = BETA_TWO * second + (1.0 - BETA_TWO) * grad * grad
    mean_hat = first_new / (1.0 - BETA_ONE**STEP)
    square_hat = second_new / (1.0 - BETA_TWO**STEP)
    weight_new = weight - rate * (mean_hat / (jnp.sqrt(square_hat) + ADAM_EPS) + decay * weight)
    return (weight_new, first_new, second_new)


def collect(tailored, qkv, out, up, down, vectors, bias):
    low = jnp.bfloat16
    attn = jnp.concatenate([qkv[0], qkv[1], qkv[2], out.T], axis=1).astype(low)
    up, down = up.astype(low), down.T.astype(low)
    if tailored:
        rows = attn.shape[0]
        small = jnp.concatenate(
            [jnp.pad(vectors, ((0, 0), (0, 128 - rows))), bias.reshape(-1, 128), jnp.zeros((5, 128))]
        ).astype(low)
        attn, up, down, small = gather(attn, up, down, small)
        vectors = jnp.swapaxes(small[:, :8, :rows], 0, 1).reshape(8, -1)
        bias = small[:, 8:11].reshape(-1)
    else:
        attn, up, down = (lax.all_gather(v, "wide", axis=0, tiled=True) for v in (attn, up, down))
        vectors = lax.all_gather(vectors.astype(low), "wide", axis=1, tiled=True)
        bias = lax.all_gather(bias.astype(low), "wide", axis=0, tiled=True)
    return attn, up, down, vectors.astype(jnp.float32), bias.astype(jnp.float32)


def total(tailored, attn, up, down, vectors, bias):
    if tailored:
        rows = attn.shape[0] // 8
        small = jnp.concatenate(
            [
                jnp.pad(jnp.swapaxes(vectors.reshape(8, 8, rows), 0, 1), ((0, 0), (0, 0), (0, 128 - rows))),
                bias.reshape(8, 3, 128),
                jnp.zeros((8, 5, 128)),
            ],
            axis=1,
        )
        own, small = reduce(attn, up, down, small)
        own = own.astype(jnp.float32)
        return own[0], own[1], own[2], small[:8, :rows], small[8:11].reshape(-1)
    attn, up, down = (
        lax.psum(lax.psum_scatter(v.astype(jnp.float32), "wide", scatter_dimension=0, tiled=True), "narrow")
        for v in (attn, up, down)
    )
    vectors = lax.psum(lax.psum_scatter(vectors, "wide", scatter_dimension=1, tiled=True), "narrow")
    bias = lax.psum(lax.psum_scatter(bias, "wide", scatter_dimension=0, tiled=True), "narrow")
    return attn, up, down, vectors, bias


def shards(
    tailored,
    tokens,
    mask_place,
    mask_count,
    masked_output_gradient,
    query_key_value_weight,
    qkv_first,
    qkv_second,
    out_weight,
    out_first,
    out_second,
    up_weight,
    up_first,
    up_second,
    down_weight,
    down_first,
    down_second_moment,
    vectors,
    vectors_first,
    vectors_second,
    up_bias,
    up_bias_first,
    up_bias_second,
):
    low = jnp.bfloat16
    seqs, length, width = tokens.shape
    slots = mask_place.shape[1]
    padded = -(-slots // 16) * 16
    flat = tokens.reshape(seqs * length, width)
    attn_w, up_w, down_w, vec, bias = collect(
        tailored, query_key_value_weight, out_weight, up_weight, down_weight, vectors, up_bias
    )
    wq, wk, wv, wo = (attn_w[:, k * width : (k + 1) * width] for k in range(4))

    query = (mm(flat, wq, NN) + vec[0]).astype(low)
    key = mm(flat, wk, NN, low)
    value = (mm(flat, wv, NN) + vec[1]).astype(low)
    query, key, value = (split_heads(v, seqs, length) for v in (query, key, value))
    mixed = lax.map(attend, (query, key, value)).reshape(seqs * length, width)

    def middle(rows, mixed):
        pre_one = rows.astype(jnp.float32) + (mm(mixed, wo, NT) + vec[2])
        hidden, normed, inverse = layer_norm(pre_one, vec[3], vec[4])
        hidden_low = hidden.astype(low)
        upper = mm(hidden_low, up_w, NN) + bias
        cumul = 0.5 * (1.0 + lax.erf(upper * SQRT_HALF))
        active = (upper * cumul).astype(low)
        pre_two = hidden + (mm(active, down_w, NT) + vec[5])
        return layer_norm(pre_two, vec[6], vec[7]), normed, inverse, hidden_low, upper, cumul, active

    layer_out = middle(flat, mixed)[0][0].astype(low).reshape(seqs, length, width)

    live = jnp.arange(padded)[None, :] < mask_count[:, None]
    spots = jnp.pad(mask_place, ((0, 0), (0, padded - slots)), constant_values=-1)
    pick = ((spots[:, :, None] == jnp.arange(length)[None, None, :]) & live[:, :, None]).astype(low)

    def take(values):
        return jnp.einsum("sil,sld->sid", pick, values.reshape(seqs, length, width), preferred_element_type=jnp.float32).astype(low)

    rows_m = take(flat).reshape(seqs * padded, width)
    mixed_m = take(mixed).reshape(seqs * padded, width)
    query_m = split_heads(take(query), seqs, padded)
    (_, normed_two, inverse_two), normed_one, inverse_one, hidden_m, upper, cumul, active = middle(rows_m, mixed_m)
    incoming = jnp.pad(masked_output_gradient.astype(jnp.float32), ((0, 0), (0, padded - slots), (0, 0)))
    incoming = jnp.where(live[:, :, None], incoming, 0.0).reshape(seqs * padded, width)
    dpre_two, dgain_two, dshift_two = norm_back(incoming, normed_two, inverse_two, vec[6])
    dbias_two = jnp.sum(dpre_two, axis=0)
    dtwo_low = dpre_two.astype(low)
    ddown = mm(dtwo_low, active, TN, low)
    dactive = mm(dtwo_low, down_w, NN)
    density = jnp.exp(-0.5 * upper * upper) * INV_ROOT_TWO_PI
    dupper = dactive * (cumul + upper * density)
    dup_bias = jnp.sum(dupper, axis=0)
    dupper_low = dupper.astype(low)
    dup = mm(hidden_m, dupper_low, TN, low)
    dhidden = dpre_two + mm(dupper_low, up_w, NT)
    dpre_one, dgain_one, dshift_one = norm_back(dhidden, normed_one, inverse_one, vec[3])
    dbias_out = jnp.sum(dpre_one, axis=0)
    done_low = dpre_one.astype(low)
    dout = mm(done_low, mixed_m, TN, low)
    dmixed = split_heads(mm(done_low, wo, NN, low), seqs, padded)
    dquery, dkey, dvalue = lax.map(attend_back, (query_m, key, value, dmixed))
    dquery = dquery.reshape(seqs * padded, width)
    dkey = dkey.reshape(seqs * length, width)
    dvalue = dvalue.reshape(seqs * length, width)
    dbias_query = jnp.sum(dquery, axis=0)
    dbias_value = jnp.sum(dvalue, axis=0)
    dquery, dkey, dvalue = dquery.astype(low), dkey.astype(low), dvalue.astype(low)
    dattn = jnp.concatenate([mm(rows_m, dquery, TN, low), mm(flat, dkey, TN, low), mm(flat, dvalue, TN, low), dout], axis=1)
    masked_part = dpre_one + mm(dquery, wq, NT)
    dtokens = jnp.einsum(
        "sil,sid->sld",
        pick.astype(jnp.float32),
        masked_part.reshape(seqs, padded, width),
        precision=lax.Precision.HIGHEST,
        preferred_element_type=jnp.float32,
    ).reshape(seqs * length, width)
    dtokens = dtokens + mm(dkey, wk, NT) + mm(dvalue, wv, NT)
    dvectors = jnp.stack(
        [dbias_query, dbias_value, dbias_out, dgain_one, dshift_one, dbias_two, dgain_two, dshift_two]
    )
    own_attn, own_up, own_down, own_vectors, own_bias = total(tailored, dattn, dup, ddown, dvectors, dup_bias)

    squares = [jnp.sum(v * v) for v in (own_attn, own_up, own_down, own_vectors, own_bias)]
    grad_norm = jnp.sqrt(lax.psum(sum(squares), "wide"))
    factor = CLIP_LIMIT / jnp.maximum(grad_norm, CLIP_LIMIT)
    own_qkv = jnp.swapaxes(own_attn[:, : 3 * width].reshape(-1, 3, width), 0, 1)
    own_out = own_attn[:, 3 * width :].T
    steps = (
        adam_step(query_key_value_weight, qkv_first, qkv_second, own_qkv, factor, DECAY_RATE, LEARN_RATE),
        adam_step(out_weight, out_first, out_second, own_out, factor, DECAY_RATE, OUTPUT_RATE),
        adam_step(up_weight, up_first, up_second, own_up, factor, DECAY_RATE, LEARN_RATE),
        adam_step(down_weight, down_first, down_second_moment, own_down.T, factor, DECAY_RATE, LEARN_RATE),
        adam_step(vectors, vectors_first, vectors_second, own_vectors, factor, 0.0, VECTOR_RATE),
        adam_step(up_bias, up_bias_first, up_bias_second, own_bias, factor, 0.0, BIAS_RATE),
    )
    return (layer_out, dtokens.reshape(seqs, length, width), grad_norm) + tuple(v for step in steps for v in step)


def solution(mesh):
    tailored = mesh.shape["wide"] == 8 and mesh.shape["narrow"] == 4
    data = P(("wide", "narrow"))
    rows = P("wide")
    columns = P(None, "wide")
    weights = (columns,) * 6 + (rows,) * 3 + (columns,) * 6 + (rows,) * 3
    return jax.shard_map(
        functools.partial(shards, tailored),
        mesh=mesh,
        in_specs=(data,) * 4 + weights,
        out_specs=(data, data, P()) + weights,
        check_vma=False,
    )
```

time: 1150 us -> 494 us (0.43)
  waiting for transfers between devices: 639 us -> 0 us
  Pallas kernels: 0 us -> 216 us
  blocking collectives: 117 us -> 17.9 us
  local copies, waits for them, and re-layouts: 93.8 us -> 38.9 us
  matrix products: 217 us -> 167 us
  other arithmetic: 57.3 us -> 41.3 us
  between operations: 21.7 us -> 6.89 us
    reduce_scatter x3 -> x0, waiting for transfers between devices: 328 us -> none  [the longest x1 164 us: shards(): lax.psum_scatter(ddown, 'wide', scatter_dimension=1, tiled=True)]
    pallas_call x0 -> x2, Pallas kernels: none -> 216 us  [the longest x1 147 us: reduce(): pl.pallas_call(functools.partial(reduce_kernel, rows), out_shape=(jax.Sha...]
    all_gather x4 -> x0, waiting for transfers between devices: 145 us -> none  [the longest x1 69.5 us: shards(): lax.all_gather(up_weight.astype(jnp.bfloat16), 'wide', axis=0, tiled=True)]
    unnamed x12 -> x0, waiting for transfers between devices: 122 us -> none
    all_gather x2 -> x0, blocking collectives: 54.3 us -> none  [the longest x1 27.8 us: shards(): lax.all_gather(up_bias.astype(jnp.bfloat16), 'wide', axis=0, tiled=True)]
    psum x1 -> x0, waiting for transfers between devices: 44.3 us -> none  [shards(): lax.psum(own_qkv.astype(jnp.bfloat16), 'narrow').astype(jnp.float32)]
    unnamed x135 -> x138, local copies, waits for them, and re-layouts: 45.8 us -> 6.74 us
    unnamed x1 -> x0, blocking collectives: 35.2 us -> none
  transfers between devices with their start and end apart: 10 -> 0, of which waited for: 8 -> 0; matrix products, arithmetic and copies ran while one was open for 23% -> 0% of each run, Pallas kernels for 0% -> 0%
where the time goes in v1:
time: 494 us; the launch traced here: 489 us
  Pallas kernels  216 us (44%)
  matrix products  167 us (34%)
  other arithmetic  41.3 us (8%)
  local copies, waits for them, and re-layouts  38.9 us (8%)
  blocking collectives  17.9 us (4%)
  between operations  6.89 us (1%)
    pallas_call x1, Pallas kernels, reduce(): pl.pallas_call(functools.partial(reduce_kernel, rows), out_shape=(jax.Sha...  147 us
    dot_general x20, matrix products, mm(): lax.dot_general(a, b, (dims, ((), ())), preferred_element_type=jnp.float32)  77.8 us
    pallas_call x1, Pallas kernels, gather(): pl.pallas_call(functools.partial(gather_kernel, rows, cols), out_shape=(f...  69 us
    sub x2, matrix products, attend(): expo = jnp.exp(raw - peak)  19.7 us
    psum x1, blocking collectives, shards(): grad_norm = jnp.sqrt(lax.psum(sum(squares), 'wide'))  17.9 us
    dot_general x2, matrix products, attend_back(): jnp.einsum('hqk,qhe->khe', dscore, query, preferred_element_type=jnp.floa...  16.8 us
    dot_general x2, matrix products, attend_back(): jnp.einsum('hqk,khe->qhe', dscore, key, preferred_element_type=jnp.float32)  16.7 us
    dot_general x2, matrix products, attend(): jnp.einsum('hqk,khe->qhe', probs, value, preferred_element_type=jnp.float32)  13.4 us

profile of v1, /device:TPU:0, one launch (start us, length us, event | category | flops | bytes accessed | tf_op | source)
XLA Modules:
  0.0 488.9 jit_solution(4138239924608859101)
XLA Ops:
  6.4 69.0 %shard_map.373 = (bf16[768,3072]{1,0:T(8,128)(2,1)}, bf16[768,3072]{1,0:T(8,128)(2,1)}, bf16[768,3072]{1,0:T(8,128)(2,1)}, bf16[8,16,128]{2,1,0:T(8,128)(2,1)}) custom-call(bf16[96,3072]{1,0:T(8,128)(2,1)} %pad_maximum_fusion.1.attn, bf16[96,3072]{1,0:T(8,128)(2,1)} %convert_element_type.160.up, bf16[96,3072]{1,0:T(8,128)(2,1)} %convert_bitcast_fusion.down, ...), custom_call_target="tpu_custom_call" | custom-call | tf_op jit(solution)/shard_map/pallas_call | solution.py:228
  90.6 3.9 fusion.135
  94.4 3.9 reshape.265
  100.0 33.5 %while.24 = (s32[]{:T(128)}, bf16[2,512,12,64]{1,3,2,0:T(8,128)(2,1)}, bf16[2,512,12,64]{1,3,2,0:T(8,128)(2,1)S(1)}, bf16[2,512,12,64]{1,3,2,0:T(8,128)(2,1)}, bf16[2,512,12,64]{1,3,2,0:T(8,128)(2,1)S(1)}, /*index=5*/s32[]{:T(128)}) while((s32[]{:T(128)}, bf16[2,512,12,64]{1,3,2,0:T(8,128)(2,1)}, bf16[2,512,12,64]{1,3,2,0:T(8,128)(2,1)S(1)}, ...), condition=%wide.region_3.4_spmd, body=%wide.region_0.3_spmd.sunk | while | flops 821428736 | bytes 28371020 | solution.py:650
  100.0 9.9 %fusion.282 = (f32[12,512]{1,0:T(8,128)S(1)}, f32[12,512,512]{1,2,0:T(8,128)}) fusion(bf16[2,512,12,64]{1,3,2,0:T(8,128)(2,1)S(1)} %get-tuple-element.434, s32[]{:T(128)S(6)} %copy.192, bf16[2,512,12,64]{1,3,2,0:T(8,128)(2,1)} %get-tuple-element.433), kind=kOutput, calls=%fused_computation.251.clone.1 | convolution fusion | flops 412090880 | bytes 14181376 | tf_op jit(solution)/shard_map/while/body/eval_jaxpr/sub | solution.py:536
  109.9 6.7 %fusion.283 = bf16[2,512,12,64]{1,3,2,0:T(8,128)(2,1)} fusion(bf16[2,512,12,64]{1,3,2,0:T(8,128)(2,1)} %get-tuple-element.425, s32[]{:T(128)S(6)} %copy.192, f32[12,512,512]{1,2,0:T(8,128)} %get-tuple-element.406, f32[12,512]{1,0:T(8,128)S(1)} %get-tuple-element.407, bf16[2,512,12,64]{1,3,2,0:T(8,128)(2,1)S(1)} %get-tuple-element.432), kind=kOutput, calls=%fused_computation.10.clone.1 | convolution fusion | flops 409337856 | bytes 14189568 | tf_op jit(solution)/shard_map/while/body/eval_jaxpr/hqk,khe->qhe/dot_general | solution.py:539
  116.6 9.8 %fusion.282 = (f32[12,512]{1,0:T(8,128)S(1)}, f32[12,512,512]{1,2,0:T(8,128)}) fusion(bf16[2,512,12,64]{1,3,2,0:T(8,128)(2,1)S(1)} %get-tuple-element.434, s32[]{:T(128)S(6)} %copy.192, bf16[2,512,12,64]{1,3,2,0:T(8,128)(2,1)} %get-tuple-element.433), kind=kOutput, calls=%fused_computation.251.clone.1 | convolution fusion | flops 412090880 | bytes 14181376 | tf_op jit(solution)/shard_map/while/body/eval_jaxpr/sub | solution.py:536
  126.4 6.7 %fusion.283 = bf16[2,512,12,64]{1,3,2,0:T(8,128)(2,1)} fusion(bf16[2,512,12,64]{1,3,2,0:T(8,128)(2,1)} %get-tuple-element.425, s32[]{:T(128)S(6)} %copy.192, f32[12,512,512]{1,2,0:T(8,128)} %get-tuple-element.406, f32[12,512]{1,0:T(8,128)S(1)} %get-tuple-element.407, bf16[2,512,12,64]{1,3,2,0:T(8,128)(2,1)S(1)} %get-tuple-element.432), kind=kOutput, calls=%fused_computation.10.clone.1 | convolution fusion | flops 409337856 | bytes 14189568 | tf_op jit(solution)/shard_map/while/body/eval_jaxpr/hqk,khe->qhe/dot_general | solution.py:539
  137.9 4.5 fusion.226
  145.0 17.7 %fusion.227 = (f32[1024]{0:T(1024)S(1)}, f32[1024,768]{1,0:T(8,128)}) fusion(f32[768]{0:T(1024)S(1)} %add.309, bf16[768,3072]{1,0:T(8,128)(2,1)} %get-tuple-element.102, f32[3072]{0:T(1024)S(1)} %reshape.277, bf16[768,3072]{1,0:T(8,128)(2,1)} %get-tuple-element.101, f32[1024,768]{1,0:T(8,128)} %get-tuple-element.321, f32[768]{0:T(1024)S(1)} %add.302, ...), kind=kOutput, calls=%fused_computation.258 | convolution fusion | flops 9691986944 | bytes 15762432 | tf_op jit(solution)/shard_map/dot_general | solution.py:518
  182.6 5.0 %fusion.225 = (f32[160]{0:T(256)S(1)}, f32[160,768]{1,0:T(8,128)S(1)}) fusion(f32[768]{0:T(1024)S(1)} %add.309, bf16[768,3072]{1,0:T(8,128)(2,1)} %get-tuple-element.102, f32[160,3072]{1,0:T(8,128)S(1)} %convolution_add_fusion, f32[768]{0:T(1024)S(1)} %add.302, f32[768]{0:T(1024)S(1)} %mul.507, f32[160]{0:T(256)S(1)} %add_rsqrt_fusion.3, ...), kind=kOutput, calls=%fused_computation.256 | convolution fusion | flops 758292352 | bytes 7678848 | tf_op jit(solution)/shard_map/dot_general | solution.py:518
  190.8 5.9 %fusion.230 = (f32[3072]{0:T(1024)}, bf16[160,3072]{1,0:T(8,128)(2,1)S(1)}) fusion(f32[160,3072]{1,0:T(8,128)} %copy-done.9, bf16[768,3072]{1,0:T(8,128)(2,1)} %get-tuple-element.102, f32[160,768]{1,0:T(8,128)S(1)} %get-tuple-element.299), kind=kOutput, calls=%fused_computation.259 | convolution fusion | flops 760501248 | bytes 8171520 | tf_op jit(solution)/shard_map/dot_general | solution.py:518
  196.8 5.2 %multiply_reduce_fusion.8 = (f32[768]{0:T(1024)}, f32[160]{0:T(256)S(1)}, f32[160]{0:T(256)S(1)}, f32[768]{0:T(1024)}, f32[160,768]{1,0:T(8,128)S(1)}) fusion(f32[160,768]{1,0:T(8,128)S(1)} %copy-done.3, f32[160]{0:T(256)S(1)} %add_rsqrt_fusion.3, f32[160]{0:T(256)S(1)} %broadcast_multiply_fusion.7, f32[768]{0:T(1024)S(1)} %mul.507, ...), kind=kOutput, calls=%fused_computation.162 | convolution fusion | flops 756201728 | bytes 7187968 | tf_op jit(solution)/shard_map/dot_general | solution.py:518
  208.7 53.0 %while.25 = (s32[]{:T(128)}, f32[2,80,12,64]{1,3,2,0:T(8,128)}, bf16[2,512,12,64]{1,3,2,0:T(8,128)(2,1)}, f32[2,512,12,64]{1,3,2,0:T(8,128)}, bf16[2,512,12,64]{...) while((s32[]{:T(128)}, f32[2,80,12,64]{1,3,2,0:T(8,128)}, ...), condition=%wide.region_20.21_spmd, body=%wide.region_16.20_spmd.sunk | while | flops 387814208 | bytes 39958172 | solution.py:693
  214.6 8.3 %fusion.299 = f32[2,80,12,64]{1,3,2,0:T(8,128)} fusion(f32[2,80,12,64]{1,3,2,0:T(8,128)} %get-tuple-element.446, s32[]{:T(128)S(6)} %copy.200, f32[12,80,512]{2,1,0:T(8,128)S(1)} %fusion.297, bf16[2,512,12,64]{1,3,2,0:T(8,128)(2,1)} %copy-done, f32[12,80,512]{2,1,0:T(8,128)} %get-tuple-element.416, f32[12,80]{1,0:T(8,128)S(1)} %get-tuple-element.417), kind=kOutput, calls=%fused_computation.39.clone.1 | convolution fusion | flops 66356672 | bytes 9061376 | tf_op jit(solution)/shard_map/while/body/eval_jaxpr/hqk,khe->qhe/dot_general | solution.py:551
  223.0 8.4 %bitcast_dynamic-update-slice_fusion.4 = bf16[2,512,12,64]{1,3,2,0:T(8,128)(2,1)} fusion(bf16[2,512,12,64]{1,3,2,0:T(8,128)(2,1)} %get-tuple-element.447, s32[]{:T(128)S(6)} %copy.200, f32[12,80,512]{2,1,0:T(8,128)S(1)} %fusion.297, bf16[2,80,12,64]{1,3,2,0:T(8,128)(2,1)} %get-tuple-element.459, f32[12,80,512]{2,1,0:T(8,128)} %get-tuple-element.416, ...), kind=kOutput, calls=%fused_computation.37.clone.1 | convolution fusion | flops 66356672 | bytes 9651200 | tf_op jit(solution)/shard_map/while/body/eval_jaxpr/hqk,qhe->khe/dot_general | solution.py:552
  240.9 8.3 %fusion.299 = f32[2,80,12,64]{1,3,2,0:T(8,128)} fusion(f32[2,80,12,64]{1,3,2,0:T(8,128)} %get-tuple-element.446, s32[]{:T(128)S(6)} %copy.200, f32[12,80,512]{2,1,0:T(8,128)S(1)} %fusion.297, bf16[2,512,12,64]{1,3,2,0:T(8,128)(2,1)} %copy-done, f32[12,80,512]{2,1,0:T(8,128)} %get-tuple-element.416, f32[12,80]{1,0:T(8,128)S(1)} %get-tuple-element.417), kind=kOutput, calls=%fused_computation.39.clone.1 | convolution fusion | flops 66356672 | bytes 9061376 | tf_op jit(solution)/shard_map/while/body/eval_jaxpr/hqk,khe->qhe/dot_general | solution.py:551
  249.3 8.4 %bitcast_dynamic-update-slice_fusion.4 = bf16[2,512,12,64]{1,3,2,0:T(8,128)(2,1)} fusion(bf16[2,512,12,64]{1,3,2,0:T(8,128)(2,1)} %get-tuple-element.447, s32[]{:T(128)S(6)} %copy.200, f32[12,80,512]{2,1,0:T(8,128)S(1)} %fusion.297, bf16[2,80,12,64]{1,3,2,0:T(8,128)(2,1)} %get-tuple-element.459, f32[12,80,512]{2,1,0:T(8,128)} %get-tuple-element.416, ...), kind=kOutput, calls=%fused_computation.37.clone.1 | convolution fusion | flops 66356672 | bytes 9651200 | tf_op jit(solution)/shard_map/while/body/eval_jaxpr/hqk,qhe->khe/dot_general | solution.py:552
  265.2 4.5 fusion.146
  278.3 4.6 fusion.115
  289.7 3.7 convolution_convert_fusion.1.g_b
  293.4 3.7 convolution_convert_fusion.g_c
  298.7 147.0 %shard_map.374 = (bf16[3,96,3072]{2,1,0:T(8,128)(2,1)}, f32[16,128]{1,0:T(8,128)}) custom-call(bf16[768,3072]{1,0:T(8,128)(2,1)} %pad_maximum_fusion.g_a, bf16[768,3072]{1,0:T(8,128)(2,1)} %convolution_convert_fusion.1.g_b, bf16[768,3072]{1,0:T(8,128)(2,1)} %convolution_convert_fusion.g_c, f32[8,16,128]{2,1,0:T(8,128)} %fusion.183.small), custom_call_target="tpu_custom_call" | custom-call | tf_op jit(solution)/shard_map/pallas_call | solution.py:473
  454.8 17.9 %psum.7 = f32[]{:T(128)} all-reduce(f32[]{:T(128)S(6)} %add.339), channel_id=1, replica_groups=mesh['wide'=8,'narrow'=4] {'wide'}, use_global_device_ids=true, to_apply=%region_35.36 | all-reduce | flops 1 | bytes 8 | tf_op jit(solution)/shard_map/psum | solution.py:716
  (261 shorter events, 118.3 us)
Async XLA Ops:
  4.8 72.5 %copy-start.24 = (bf16[2,512,768]{2,1,0:T(8,128)(2,1)S(1)}, bf16[2,512,768]{2,1,0:T(8,128)(2,1)}, u32[]{:S(2)}) copy-start(bf16[2,512,768]{2,1,0:T(8,128)(2,1)} %param.26) | copy-start | bytes 4718596
  85.1 5.5 %copy-start.11 = (bf16[1024,768]{0,1:T(8,128)(2,1)}, bf16[1024,768]{0,1:T(8,128)(2,1)S(1)}, u32[]{:S(2)}) copy-start(bf16[1024,768]{0,1:T(8,128)(2,1)S(1)} %fusion.137) | copy-start | bytes 4718596
  170.0 5.1 %copy-start.47 = (s32[2,80]{1,0:T(2,128)}, s32[2,80]{1,0:T(2,128)S(1)}, u32[]{:S(2)}) copy-start(s32[2,80]{1,0:T(2,128)S(1)} %pad.21) | copy-start | bytes 1924
  170.1 5.0 %copy-start.58 = (pred[2,80]{1,0:T(4,128)(4,1)}, pred[2,80]{1,0:T(4,128)(4,1)S(1)}, u32[]{:S(2)}) copy-start(pred[2,80]{1,0:T(4,128)(4,1)S(1)} %copy.150) | copy-start | bytes 484
  177.6 5.1 %copy-start.2 = (f32[160,768]{1,0:T(8,128)}, f32[160,768]{1,0:T(8,128)S(1)}, u32[]{:S(2)}) copy-start(f32[160,768]{1,0:T(8,128)S(1)} %get-tuple-element.316) | copy-start | bytes 1474564
  177.6 24.4 %copy-start.43 = (f32[160]{0:T(256)}, f32[160]{0:T(256)S(1)}, u32[]{:S(2)}) copy-start(f32[160]{0:T(256)S(1)} %broadcast_multiply_fusion.7) | copy-start | bytes 1924
  177.8 24.1 %copy-start.45 = (f32[160]{0:T(256)}, f32[160]{0:T(256)S(1)}, u32[]{:S(2)}) copy-start(f32[160]{0:T(256)S(1)} %add_rsqrt_fusion.3) | copy-start | bytes 1924
  179.1 8.8 %copy-start.8 = (f32[2,80,768]{2,1,0:T(8,128)}, f32[2,80,768]{2,1,0:T(8,128)S(1)}, u32[]{:S(2)}) copy-start(f32[2,80,768]{2,1,0:T(8,128)S(1)} %copy.152) | copy-start | bytes 1474564
  182.6 5.0 %copy-start.9 = (f32[160,3072]{1,0:T(8,128)}, f32[160,3072]{1,0:T(8,128)S(1)}, u32[]{:S(2)}) copy-start(f32[160,3072]{1,0:T(8,128)S(1)} %convolution_add_fusion) | copy-start | bytes 5898244
  190.8 5.9 %copy-start.12 = (f32[160,768]{1,0:T(8,128)}, f32[160,768]{1,0:T(8,128)S(1)}, u32[]{:S(2)}) copy-start(f32[160,768]{1,0:T(8,128)S(1)} %get-tuple-element.299) | copy-start | bytes 1474564
  190.8 5.9 %copy-start.3 = (f32[160,768]{1,0:T(8,128)S(1)}, f32[160,768]{1,0:T(8,128)}, u32[]{:S(2)}) copy-start(f32[160,768]{1,0:T(8,128)} %copy-done.2) | copy-start | bytes 1474564
  196.8 5.2 %copy-start.19 = (bf16[160,3072]{1,0:T(8,128)(2,1)}, bf16[160,3072]{1,0:T(8,128)(2,1)S(1)}, u32[]{:S(2)}) copy-start(bf16[160,3072]{1,0:T(8,128)(2,1)S(1)} %get-tuple-element.325) | copy-start | bytes 2949124
  265.1 4.5 copy-start.39
  278.3 4.6 copy-start.37
  278.3 5.1 %copy-start.28 = (bf16[2,512,768]{2,1,0:T(8,128)(2,1)S(1)}, bf16[2,512,768]{2,1,0:T(8,128)(2,1)}, u32[]{:S(2)}) copy-start(bf16[2,512,768]{2,1,0:T(8,128)(2,1)} %param.26) | copy-start | bytes 4718596
  293.4 3.9 copy-start.55
  293.4 4.0 copy-start.51
  293.4 4.1 copy-start.50
  293.4 4.1 copy-start.54
  293.4 4.2 copy-start.53
  293.4 4.3 copy-start.52
  293.4 4.4 copy-start.60
  475.1 5.5 %copy-start.30 = (f32[96,3072]{1,0:T(8,128)S(1)}, f32[96,3072]{1,0:T(8,128)}, u32[]{:S(2)}) copy-start(f32[96,3072]{1,0:T(8,128)} %param.37) | copy-start | bytes 3538948
  475.1 5.5 %copy-start.31 = (f32[96,3072]{1,0:T(8,128)S(1)}, f32[96,3072]{1,0:T(8,128)}, u32[]{:S(2)}) copy-start(f32[96,3072]{1,0:T(8,128)} %param.38) | copy-start | bytes 3538948
  (47 other events, 115.1 us)
